TPU v7x, 32 devices: a whole 2x2x4 slice. The times are simulated.
32 devices in a mesh: flux: 4 (over z), obs: 8 (over y, x, core).
Axes of the slice: x: 2, y: 2, z: 4, core: 2. Of those that a mesh axis runs over, the one named last changes fastest.
Arguments:
- footprint: bfloat16 [256, 4, 4, 2, 4096], P(('flux', 'obs')), may hold values from 0.00049972534 to 0.049804688
- obs_hour: int32 [256, 4], P(('flux', 'obs')), may hold values from 0 to 3
- tile_list: int32 [256, 4], P(('flux', 'obs')), may hold values from 0 to 511, as said below
- tile_row: int32 [512], replicated, may hold values from 0 to 511, as said below
- flux: bfloat16 [512, 5, 4096], P('flux'), may hold values from -6 to 6
- observed: float32 [256, 4], P(('flux', 'obs')), may hold values from -18 to 18
- obs_var: float32 [256, 4], P(('flux', 'obs')), may hold values from 0.5 to 4
Outputs:
- modeled: float32 [256, 4], P(('flux', 'obs'))
- gradient: float32 [512, 5, 4096], P('flux', None, 'obs')
Inputs may be any that keep to these rules, and one draw needn't show every extreme that they name: `tile_row`: A permutation: every tile has its own storage row, and the row r lies on index r // 128 of flux. `tile_list`: among the 32 listed tiles of one device's 8 blocks, at most 16 have storage rows on one index of flux; on every device some index of flux gets exactly 16.
All inputs are finite; a program needn't handle non-finite values.
Results may differ from a plain program's by a relative error of at most 0.0019.
Values may be sent and summed in bfloat16 or wider, within the bound.
No kernel may reach another device: no remote copies, remote signals or barrier semaphores. Data moves between devices by JAX's collectives and lax.ppermute only.
A program may use at most 64 MiB of HBM per device.

v0:
```python
import jax
import jax.numpy as jnp
from jax import lax
from jax.sharding import PartitionSpec as P


def hour_select(hour_rows, lag_count, hour_count):
    target = hour_rows[:, :, None] + jnp.arange(lag_count, dtype=jnp.int32)[None, None, :]
    return (target[..., None] == jnp.arange(hour_count, dtype=jnp.int32)).astype(jnp.float32)


def forward_terms(footprints, windows, select):
    products = jnp.einsum("nolc,nhc->nolh", footprints, windows, preferred_element_type=jnp.float32)
    return jnp.sum(products * select, axis=(2, 3))


def adjoint_terms(select, scaled, footprints):
    coefficient = (select * scaled.astype(jnp.float32)[:, :, None, None]).astype(jnp.bfloat16)
    return jnp.einsum("nolh,nolc->nhc", coefficient, footprints, preferred_element_type=jnp.float32)


def fetch_windows(flux, wanted):
    present = (wanted >= 0).astype(flux.dtype)
    rows_taken = jnp.take(flux, jnp.maximum(wanted, 0), axis=0)
    return rows_taken * present[:, None, None]


def accumulate(wanted, gradients, tile_count):
    onehot = (wanted[None, :] == jnp.arange(tile_count, dtype=jnp.int32)[:, None]).astype(
        jnp.float32
    )
    flattened = gradients.reshape(gradients.shape[0], gradients.shape[1] * gradients.shape[2])
    summed = jnp.dot(
        onehot, flattened, precision=lax.Precision.HIGHEST, preferred_element_type=jnp.float32
    )
    return summed.reshape(tile_count, gradients.shape[1], gradients.shape[2])


def shards(footprint, obs_hour, tile_list, tile_row, flux, observed, obs_var):
    owners = lax.axis_size("flux")
    block_count, slot_width, sounding_count, lag_count, cell_count = footprint.shape
    tile_count = flux.shape[0]
    hour_count = flux.shape[1]
    slot_count = block_count * slot_width
    capacity = 2 * slot_count // owners
    buffer_size = owners * capacity
    listed = tile_list.reshape(slot_count)
    table_hits = listed[:, None] == jnp.arange(tile_row.shape[0], dtype=jnp.int32)[None, :]
    storage = jnp.sum(jnp.where(table_hits, tile_row[None, :], 0), axis=1)
    owner_index = storage // tile_count
    local_index = storage % tile_count
    slot_iota = jnp.arange(slot_count, dtype=jnp.int32)
    earlier = (owner_index[:, None] == owner_index[None, :]) & (
        slot_iota[None, :] < slot_iota[:, None]
    )
    position = owner_index * capacity + jnp.sum(earlier.astype(jnp.int32), axis=1)
    matches = position[None, :] == jnp.arange(buffer_size, dtype=jnp.int32)[:, None]
    filled = jnp.any(matches, axis=1)
    source = jnp.sum(jnp.where(matches, slot_iota[None, :], 0), axis=1)
    requests = jnp.where(filled, local_index[source], -1).reshape(owners, capacity)
    select = hour_select(obs_hour, lag_count, hour_count)
    slot_select = jnp.broadcast_to(
        select[:, None], (block_count, slot_width, sounding_count, lag_count, hour_count)
    ).reshape(slot_count, sounding_count, lag_count, hour_count)
    slot_feet = footprint.reshape(slot_count, sounding_count, lag_count, cell_count)
    incoming = lax.all_to_all(requests, "flux", split_axis=0, concat_axis=0, tiled=True)
    served = fetch_windows(flux, incoming.reshape(buffer_size)).reshape(
        owners, capacity, hour_count, cell_count
    )
    arrived = lax.all_to_all(served, "flux", split_axis=0, concat_axis=0, tiled=True).reshape(
        buffer_size, hour_count, cell_count
    )
    slot_tiles = jnp.take(arrived, position, axis=0)
    partial_value = forward_terms(slot_feet, slot_tiles, slot_select).reshape(
        block_count, slot_width, sounding_count
    )
    modeled = jnp.sum(partial_value, axis=1)
    scaled = ((modeled - observed) / obs_var).astype(jnp.bfloat16)
    slot_scaled = jnp.broadcast_to(
        scaled[:, None], (block_count, slot_width, sounding_count)
    ).reshape(slot_count, sounding_count)
    gradients = adjoint_terms(slot_select, slot_scaled, slot_feet)
    outgoing = jnp.take(gradients, source, axis=0) * filled.astype(jnp.float32)[:, None, None]
    returned = lax.all_to_all(
        outgoing.reshape(owners, capacity, hour_count, cell_count),
        "flux",
        split_axis=0,
        concat_axis=0,
        tiled=True,
    )
    local_sum = accumulate(
        incoming.reshape(buffer_size),
        returned.reshape(buffer_size, hour_count, cell_count),
        tile_count,
    )
    gradient = lax.psum_scatter(local_sum, "obs", scatter_dimension=2, tiled=True)
    return (modeled, gradient)


def solution(mesh):
    placed = (
        P(("flux", "obs"), None, None, None, None),
        P(("flux", "obs"), None),
        P(("flux", "obs"), None),
        P(),
        P("flux", None, None),
        P(("flux", "obs"), None),
        P(("flux", "obs"), None),
    )
    return jax.shard_map(
        shards,
        mesh=mesh,
        in_specs=placed,
        out_specs=(P(("flux", "obs"), None), P("flux", None, "obs")),
        check_vma=False,
    )
```

profile of v0, /device:TPU:0, one launch (start us, length us, event | category | flops | bytes accessed | tf_op | source)
XLA Modules:
  0.0 358.4 jit_solution(2463976118220577694)
XLA Ops:
  7.2 0.0 copy-start
  7.2 0.9 copy.45
  8.1 0.1 eq.73
  8.2 0.9 select_reduce_fusion
  9.0 0.2 convert_reduce_fusion
  9.2 0.1 fusion.32
  9.3 0.1 select_reduce_fusion.1
  9.5 0.8 gather_fusion
  10.2 0.1 select_n.112
  10.3 11.7 %all_to_all.16 = s32[4,1,16]{2,1,0:T(1,128)S(1)} all-to-all(s32[4,1,16]{2,1,0:T(1,128)S(1)} %bitcast.79), channel_id=1, replica_groups=mesh['flux'=4,'obs'=8] {'flux'}, dimensions={0} | all-to-all | bytes 512 | tf_op jit(solution)/shard_map/all_to_all | solution.py:66
  22.0 0.5 broadcast.309
  22.5 0.7 fusion.39
  23.2 0.1 reshape.252
  23.3 14.2 %gather_fusion.1 = bf16[64,5,4096]{2,0,1:T(8,128)(2,1)} fusion(bf16[128,5,4096]{2,0,1:T(8,128)(2,1)} %param.11, s32[1024]{0:T(1024)S(1)} %pad_clamp_fusion.1), kind=kCustom, calls=%fused_computation.1 | custom fusion | bytes 5243136 | tf_op jit(solution)/shard_map/jit(_take)/gather | solution.py:24
  37.5 0.0 copy-start.2
  37.5 3.6 fusion.4
  41.1 4.7 %all-to-all-start.1 = ((bf16[4,16,5,4096]{3,1,2,0:T(8,128)(2,1)}), bf16[4,16,5,4096]{3,1,2,0:T(8,128)(2,1)}, u32[]{:S(2)}, u32[]{:S(2)}) async-start(bf16[4,16,5,4096]{3,1,2,0:T(8,128)(2,1)} %fusion.4), calls=%async_computation.1 | async-start | bytes 5242880 | tf_op jit(solution)/shard_map/all_to_all | solution.py:70
  45.8 0.1 reduce_sum.61
  45.9 0.0 copy-done.2
  45.9 0.1 copy.50
  46.0 0.1 reshape.241
  46.1 0.1 fusion.28
  46.2 56.4 %all-to-all-done.1 = bf16[4,16,5,4096]{3,1,2,0:T(8,128)(2,1)} async-done(((bf16[4,16,5,4096]{3,1,2,0:T(8,128)(2,1)}), bf16[4,16,5,4096]{3,1,2,0:T(8,128)(2,1)}, u32[]{:S(2)}, u32[]{:S(2)}) %all-to-all-start.1) | async-done | bytes 2621472 | tf_op jit(solution)/shard_map/all_to_all | solution.py:70
  102.6 5.3 %copy.48 = bf16[4,16,5,4096]{3,2,1,0:T(8,128)(2,1)} copy(bf16[4,16,5,4096]{3,1,2,0:T(8,128)(2,1)} %all-to-all-done.1) | data formatting | bytes 5242880 | tf_op jit(solution)/shard_map/all_to_all | solution.py:70
  107.9 4.2 %gather_fusion.2 = bf16[32,5,4096]{2,1,0:T(8,128)(2,1)} fusion(bf16[64,5,4096]{2,1,0:T(8,128)(2,1)} %bitcast.74, s32[1024]{0:T(1024)S(1)} %pad_clamp_fusion), kind=kCustom, calls=%fused_computation.2 | custom fusion | bytes 2621568 | tf_op jit(solution)/shard_map/jit(_take)/gather | solution.py:73
  112.1 0.0 copy-done
  112.2 0.0 copy-start.3
  112.2 0.0 copy-start.4
  112.2 3.7 %fusion.21 = f32[32,4]{1,0:T(8,128)S(1)} fusion(f32[32,4,2,5]{3,1,2,0:T(4,128)S(1)} %bitcast.75, bf16[32,4,2,4096]{3,2,1,0:T(2,128)(2,1)S(1)} %bitcast.69, bf16[32,5,4096]{2,1,0:T(8,128)(2,1)} %gather_fusion.2, pred[32]{0:T(512)(128)(4,1)S(1)} %get-tuple-element.4), kind=kOutput, calls=%fused_computation.20 | convolution fusion | flops 11143552 | bytes 3413536 | tf_op jit(solution)/shard_map/nolc,nhc->nolh/dot_general | solution.py:13
  115.9 0.1 copy.63
  116.0 0.0 copy-done.3
  116.0 0.0 copy-done.4
  116.0 0.0 copy-start.1
  116.0 0.1 copy.64
  116.1 3.6 convolution_bitcast_fusion
  119.7 6.5 %gather_fusion.3 = f32[64,5,4096]{2,1,0:T(8,128)} fusion(f32[32,5,4096]{2,1,0:T(8,128)} %convolution_bitcast_fusion, s32[1024]{0:T(1024)S(1)} %pad_clamp_fusion.2), kind=kCustom, calls=%fused_computation.3 | custom fusion | bytes 10486016 | tf_op jit(solution)/shard_map/jit(_take)/gather | solution.py:83
  126.2 0.0 copy-done.1
  126.2 9.1 %fusion.3 = f32[4,16,5,4096]{3,1,2,0:T(8,128)} fusion(f32[4,16,5,4096]{3,2,1,0:T(8,128)} %bitcast.71, f32[4,16]{1,0:T(4,128)S(1)} %reshape.241, pred[4,16]{1,0:T(4,128)(4,1)S(1)} %compare_and_fusion), kind=kLoop, calls=%fused_computation.9 | loop fusion | flops 2621440 | bytes 10486080 | tf_op jit(solution)/shard_map/mul | solution.py:83
  135.3 5.0 %all-to-all-start.2 = ((f32[4,16,5,4096]{3,1,2,0:T(8,128)}), f32[4,16,5,4096]{3,1,2,0:T(8,128)}, u32[]{:S(2)}, u32[]{:S(2)}) async-start(f32[4,16,5,4096]{3,1,2,0:T(8,128)} %fusion.3), calls=%async_computation.2 | async-start | bytes 10485760 | tf_op jit(solution)/shard_map/all_to_all | solution.py:84
  140.3 0.3 reduce-scatter.2.cloned.1.call-start
  140.6 0.1 reshape.239
  140.7 114.8 %all-to-all-done.2 = f32[4,16,5,4096]{3,1,2,0:T(8,128)} async-done(((f32[4,16,5,4096]{3,1,2,0:T(8,128)}), f32[4,16,5,4096]{3,1,2,0:T(8,128)}, u32[]{:S(2)}, u32[]{:S(2)}) %all-to-all-start.2) | async-done | bytes 5242912 | tf_op jit(solution)/shard_map/all_to_all | solution.py:84
  255.5 5.7 %copy.55 = f32[4,16,5,4096]{3,2,1,0:T(8,128)S(1)} copy(f32[4,16,5,4096]{3,1,2,0:T(8,128)} %all-to-all-done.2) | data formatting | bytes 10485760 | tf_op jit(solution)/shard_map/all_to_all | solution.py:84
  261.2 9.3 %fusion = f32[128,5,4096]{2,0,1:T(8,128)} fusion(s32[64]{0:T(128)S(1)} %reshape.239, f32[8,8,5,4096]{3,2,1,0:T(8,128)S(1)} %bitcast.72), kind=kOutput, calls=%fused_computation.5 | convolution fusion | flops 2013274112 | bytes 15728896 | tf_op jit(solution)/shard_map/dot_general | solution.py:33
  270.6 0.0 reduce-scatter.2.cloned.1.call-update
  270.6 81.0 %reduce-scatter.2.cloned.1.call-done = f32[128,5,512]{2,0,1:T(8,128)} async-done(((f32[128,5,4096]{2,0,1:T(8,128)}), f32[128,5,512]{2,0,1:T(8,128)}) %reduce-scatter.2.cloned.1.call-update) | async-done | bytes 1310736 | tf_op jit(solution)/shard_map/reduce_scatter | solution.py:96
  (18 shorter events, 0.2 us)
Async XLA Ops:
  7.2 105.0 %copy-start = (bf16[8,4,4,2,4096]{4,3,2,1,0:T(2,128)(2,1)S(1)}, bf16[8,4,4,2,4096]{4,3,2,1,0:T(2,128)(2,1)}, u32[]{:S(2)}) copy-start(bf16[8,4,4,2,4096]{4,3,2,1,0:T(2,128)(2,1)} %param.7) | copy-start | bytes 6291460
  37.5 8.4 %copy-start.2 = (s32[8,4]{0,1:T(4,128)S(1)}, s32[8,4]{0,1:T(4,128)}, u32[]{:S(2)}) copy-start(s32[8,4]{0,1:T(4,128)} %param.8) | copy-start | bytes 388
  41.1 61.6 %all-to-all-start.1 = ((bf16[4,16,5,4096]{3,1,2,0:T(8,128)(2,1)}), bf16[4,16,5,4096]{3,1,2,0:T(8,128)(2,1)}, u32[]{:S(2)}, u32[]{:S(2)}) async-start(bf16[4,16,5,4096]{3,1,2,0:T(8,128)(2,1)} %fusion.4), calls=%async_computation.1 | async-start | bytes 5242880 | tf_op jit(solution)/shard_map/all_to_all | solution.py:70
  112.2 3.9 %copy-start.3 = (f32[8,4]{0,1:T(4,128)S(1)}, f32[8,4]{0,1:T(4,128)}, u32[]{:S(2)}) copy-start(f32[8,4]{0,1:T(4,128)} %param.13) | copy-start | bytes 388
  112.2 3.9 %copy-start.4 = (f32[8,4]{0,1:T(4,128)S(1)}, f32[8,4]{0,1:T(4,128)}, u32[]{:S(2)}) copy-start(f32[8,4]{0,1:T(4,128)} %param.12) | copy-start | bytes 388
  116.0 10.2 %copy-start.1 = (f32[8,4]{0,1:T(4,128)}, f32[8,4]{0,1:T(4,128)S(1)}, u32[]{:S(2)}) copy-start(f32[8,4]{0,1:T(4,128)S(1)} %copy.63) | copy-start | bytes 388
  135.3 120.2 %all-to-all-start.2 = ((f32[4,16,5,4096]{3,1,2,0:T(8,128)}), f32[4,16,5,4096]{3,1,2,0:T(8,128)}, u32[]{:S(2)}, u32[]{:S(2)}) async-start(f32[4,16,5,4096]{3,1,2,0:T(8,128)} %fusion.3), calls=%async_computation.2 | async-start | bytes 10485760 | tf_op jit(solution)/shard_map/all_to_all | solution.py:84
  140.3 211.2 %reduce-scatter.2.cloned.1.call-start = ((), (), s32[]{:S(2)}) async-start(), calls=%async_computation.4 | async-start | bytes 11796480 | tf_op jit(solution)/shard_map/reduce_scatter | solution.py:96
Sparse Core Ops, SparseCore 0:
  270.7 80.8 reduce-scatter.1
where the time goes:
time: 360 us; the launch traced here: 358 us
  waiting for transfers between devices  252 us (70%)
  local copies, waits for them, and re-layouts  38.9 us (11%)
  matrix products  16.7 us (5%)
  other arithmetic  14.7 us (4%)
  between operations  14.2 us (4%)
  blocking collectives  11.7 us (3%)
  starting transfers between devices  10 us (3%)
    all_to_all x1, waiting for transfers between devices, shards(): lax.all_to_all(outgoing.reshape(owners, capacity, hour_count, cell_count)...  115 us
    reduce_scatter x1, waiting for transfers between devices, shards(): lax.psum_scatter(local_sum, 'obs', scatter_dimension=2, tiled=True)  81 us
    all_to_all x1, waiting for transfers between devices, shards(): lax.all_to_all(served, 'flux', split_axis=0, concat_axis=0, tiled=True)  56.4 us
    gather x1, local copies, waits for them, and re-layouts, fetch_windows(): rows_taken = jnp.take(flux, jnp.maximum(wanted, 0), axis=0)  14.2 us
    all_to_all x1, blocking collectives, shards(): lax.all_to_all(requests, 'flux', split_axis=0, concat_axis=0, tiled=True)  11.7 us
    dot_general x1, matrix products, accumulate(): jnp.dot(onehot, flattened, precision=lax.Precision.HIGHEST, preferred_ele...  9.34 us
    mul x1, other arithmetic, shards(): jnp.take(gradients, source, axis=0)  9.07 us
  transfers between devices with their start and end apart: 3, of which 3 were waited for; matrix products, arithmetic and copies ran while one was open for 0% of the time, Pallas kernels for 0%

commit v1 on v0

v1 whole, which is shorter than its diff:
```python
import functools

import jax
import jax.numpy as jnp
from jax import lax
from jax.experimental import pallas as pl
from jax.experimental.pallas import tpu as pltpu
from jax.sharding import PartitionSpec as P

LANES = 128
VMEM_BYTES = 48 * 1024 * 1024


def iota(shape, dim):
    return lax.broadcasted_iota(jnp.int32, shape, dim)


def pack_kernel(
    dims, list_ref, row_ref, hour_ref, seen_ref, var_ref, feet_ref, send_ref, meta_ref, place, count
):
    owners, columns, capacity, tiles, blocks, width, soundings, lags = dims
    per_slot = soundings * lags
    rows = capacity * per_slot

    @pl.when(pl.program_id(0) == 0)
    def _():
        shape = (owners * rows // LANES, LANES)
        flat = iota(shape, 0) * LANES + iota(shape, 1)
        slot_at, inner = flat // per_slot, flat % per_slot
        sounding, lag = inner // lags, inner % lags
        key_at = iota((1, blocks * width * per_slot), 1)
        key = jnp.zeros(key_at.shape, jnp.int32)
        target = jnp.full(shape, -1, jnp.int32)
        index = jnp.full(shape, -1, jnp.int32)
        seen = jnp.zeros(shape, jnp.float32)
        spread = jnp.ones(shape, jnp.float32)
        for o in range(owners):
            count[o] = 0
        for b in range(blocks):
            hours = jnp.zeros(shape, jnp.int32)
            block_seen = jnp.zeros(shape, jnp.float32)
            block_var = jnp.ones(shape, jnp.float32)
            for o in range(soundings):
                here = sounding == o
                hours = jnp.where(here, (hour_ref[o, b] + lag) * tiles, hours)
                block_seen = jnp.where(here, seen_ref[o, b], block_seen)
                block_var = jnp.where(here, var_ref[o, b], block_var)
            for k in range(width):
                stored = row_ref[list_ref[k, b]]
                owner = lax.div(stored, jnp.int32(tiles))
                position = count[owner]
                count[owner] = position + 1
                goes = owner * capacity + position
                here = slot_at == goes
                target = jnp.where(here, hours + (stored - owner * tiles), target)
                index = jnp.where(here, b * soundings + sounding, index)
                seen = jnp.where(here, block_seen, seen)
                spread = jnp.where(here, block_var, spread)
                key = jnp.where(
                    key_at // per_slot == b * width + k, goes * per_slot + key_at % per_slot, key
                )
        place[...] = (iota(place.shape, 0) == key).astype(jnp.bfloat16)
        fields = (target.astype(jnp.float32), index.astype(jnp.float32), seen, spread)
        for o in range(owners):
            first = o * rows
            for f, field in enumerate(fields):
                part = field[
                    first // LANES : first // LANES + 1, first % LANES : first % LANES + rows
                ]
                meta_ref[o, :, f, :] = jnp.broadcast_to(part, (columns, rows))

    packed = jnp.dot(place[...], feet_ref[...], preferred_element_type=jnp.float32)
    send_ref[...] = packed.astype(jnp.bfloat16).reshape(send_ref.shape)


def forward_kernel(dims, at_ref, meta_ref, flux_ref, feet_ref, out_ref, acc):
    rows, copies, devices, states = dims
    step = pl.program_id(0)
    hours, tiles, cells = flux_ref.shape
    pieces = feet_ref.shape[0] // LANES
    per_piece = LANES // rows
    lane = iota((8, LANES), 1)

    @pl.when(step == 0)
    def _():
        acc[...] = jnp.zeros_like(acc)

    products = lax.dot_general(
        flux_ref[...].reshape(hours * tiles, cells),
        feet_ref[...],
        (((1,), (1,)), ((), ())),
        preferred_element_type=jnp.float32,
    )
    level = iota((hours * tiles, LANES), 0)
    for n in range(pieces):
        piece = step * pieces + n
        target = meta_ref[0, pl.ds(piece, 1), :].astype(jnp.int32)
        index = meta_ref[1, pl.ds(piece, 1), :].astype(jnp.int32)
        chosen = jnp.where(level == target, products[:, n * LANES : (n + 1) * LANES], 0.0)
        partial = jnp.sum(chosen, axis=0, keepdims=True)
        for part in range(per_piece):
            device = piece * per_piece + part
            block = pl.ds(pl.multiple_of(device // 32 * 8, 8), 8)
            total = acc[block, :]
            for q in range(states // 8):
                mine = (index == q * 8 + iota((8, LANES), 0)) & (lane // rows == part)
                column = jnp.sum(jnp.where(mine, partial, 0.0), axis=1, keepdims=True)
                total = jnp.where(lane == q * 32 + device % 32, column, total)
            acc[block, :] = total

    @pl.when(step == pl.num_programs(0) - 1)
    def _():
        out_ref[...] = jnp.broadcast_to(acc[...][None], out_ref.shape)


def adjoint_kernel(dims, at_ref, sums_ref, meta_ref, feet_ref, modeled_ref, grad_ref, model, coef):
    rows, devices, states, soundings = dims
    step = pl.program_id(0)
    hours, tiles, cells = grad_ref.shape
    pieces = feet_ref.shape[0] // LANES
    per_piece = LANES // rows
    lane = iota((8, LANES), 1)

    @pl.when(step == 0)
    def _():
        model[...] = jnp.sum(sums_ref[...], axis=0)
        me = at_ref[0]
        own = model[pl.ds(pl.multiple_of(me // 32 * 8, 8), 8), :]
        result = jnp.zeros(modeled_ref.shape, jnp.float32)
        at_block = iota(modeled_ref.shape, 1)
        for q in range(states // 8):
            column = jnp.sum(
                jnp.where(lane == q * 32 + me % 32, own, 0.0), axis=1, keepdims=True
            )
            for half in range(8 // soundings):
                part = column[half * soundings : (half + 1) * soundings]
                result = jnp.where(at_block == q * (8 // soundings) + half, part, result)
        modeled_ref[...] = result

    level = iota((hours * tiles, LANES), 0)
    for n in range(pieces):
        piece = step * pieces + n
        target = meta_ref[0, pl.ds(piece, 1), :].astype(jnp.int32)
        index = meta_ref[1, pl.ds(piece, 1), :].astype(jnp.int32)
        gathered = jnp.zeros((8, LANES), jnp.float32)
        for part in range(per_piece):
            device = piece * per_piece + part
            block = model[pl.ds(pl.multiple_of(device // 32 * 8, 8), 8), :]
            for q in range(states // 8):
                column = jnp.sum(
                    jnp.where(lane == q * 32 + device % 32, block, 0.0), axis=1, keepdims=True
                )
                mine = (index == q * 8 + iota((8, LANES), 0)) & (lane // rows == part)
                gathered = jnp.where(mine, column, gathered)
        value = jnp.sum(gathered, axis=0, keepdims=True)
        seen = meta_ref[2, pl.ds(piece, 1), :]
        spread = meta_ref[3, pl.ds(piece, 1), :]
        scaled = ((value - seen) / spread).astype(jnp.bfloat16).astype(jnp.float32)
        coef[:, n * LANES : (n + 1) * LANES] = jnp.where(level == target, scaled, 0.0).astype(
            jnp.bfloat16
        )
    terms = jnp.dot(coef[...], feet_ref[...], preferred_element_type=jnp.float32)
    terms = terms.reshape(grad_ref.shape)

    @pl.when(step == 0)
    def _():
        grad_ref[...] = terms

    @pl.when(step > 0)
    def _():
        grad_ref[...] += terms


def shards(footprint, obs_hour, tile_list, tile_row, flux, observed, obs_var):
    owners, columns = lax.axis_size("flux"), lax.axis_size("obs")
    devices = owners * columns
    blocks, width, soundings, lags, cells = footprint.shape
    tiles, hours = flux.shape[:2]
    capacity = 2 * blocks * width // owners
    per_slot = soundings * lags
    rows = capacity * per_slot
    part = cells // columns
    states = blocks * soundings
    both = ("flux", "obs")
    params = pltpu.CompilerParams(vmem_limit_bytes=VMEM_BYTES)
    smem = pl.BlockSpec(memory_space=pltpu.SMEM)

    send, meta = pl.pallas_call(
        functools.partial(
            pack_kernel, (owners, columns, capacity, tiles, blocks, width, soundings, lags)
        ),
        grid=(columns,),
        out_shape=(
            jax.ShapeDtypeStruct((owners, columns, rows, part), jnp.bfloat16),
            jax.ShapeDtypeStruct((owners, columns, 4, rows), jnp.float32),
        ),
        in_specs=[smem] * 5
        + [pl.BlockSpec((blocks * width * per_slot, part), lambda j: (0, j))],
        out_specs=(
            pl.BlockSpec((owners, 1, rows, part), lambda j: (0, j, 0, 0)),
            pl.BlockSpec((owners, columns, 4, rows), lambda j: (0, 0, 0, 0)),
        ),
        scratch_shapes=[
            pltpu.VMEM((owners * rows, blocks * width * per_slot), jnp.bfloat16),
            pltpu.SMEM((owners,), jnp.int32),
        ],
        compiler_params=params,
        name="pack",
    )(
        tile_list.T,
        tile_row,
        obs_hour.T,
        observed.T,
        obs_var.T,
        footprint.reshape(blocks * width * per_slot, cells),
    )
    feet = lax.all_to_all(
        send.reshape(devices, rows, part), both, split_axis=0, concat_axis=0, tiled=True
    ).reshape(devices * rows, part)
    meta = lax.all_to_all(
        meta.reshape(devices, 4, rows), both, split_axis=0, concat_axis=0, tiled=True
    )
    meta = meta.transpose(1, 0, 2).reshape(4, devices * rows // LANES, LANES)

    total = devices * rows
    chunk = min(1024, total)
    pages = states * devices // LANES
    one_shot = devices <= 64
    copies = devices if one_shot else 1
    at = jnp.stack([lax.axis_index("flux") * columns + lax.axis_index("obs"), lax.axis_index("obs")])
    sums = pl.pallas_call(
        functools.partial(forward_kernel, (rows, copies, devices, states)),
        grid_spec=pltpu.PrefetchScalarGridSpec(
            num_scalar_prefetch=1,
            grid=(total // chunk,),
            in_specs=[
                pl.BlockSpec(meta.shape, lambda i, at: (0, 0, 0)),
                pl.BlockSpec((hours, tiles, part), lambda i, at: (0, 0, at[1])),
                pl.BlockSpec((chunk, part), lambda i, at: (i, 0)),
            ],
            out_specs=pl.BlockSpec((copies, pages, LANES), lambda i, at: (0, 0, 0)),
            scratch_shapes=[pltpu.VMEM((pages, LANES), jnp.float32)],
        ),
        out_shape=jax.ShapeDtypeStruct((copies, pages, LANES), jnp.float32),
        compiler_params=params,
        name="forward",
    )(at, meta, flux.transpose(1, 0, 2), feet)
    if one_shot:
        sums = lax.all_to_all(sums, both, split_axis=0, concat_axis=0, tiled=True)
    else:
        sums = lax.psum(sums, both)
    modeled, gradient = pl.pallas_call(
        functools.partial(adjoint_kernel, (rows, devices, states, soundings)),
        grid_spec=pltpu.PrefetchScalarGridSpec(
            num_scalar_prefetch=1,
            grid=(total // chunk,),
            in_specs=[
                pl.BlockSpec((copies, pages, LANES), lambda i, at: (0, 0, 0)),
                pl.BlockSpec(meta.shape, lambda i, at: (0, 0, 0)),
                pl.BlockSpec((chunk, part), lambda i, at: (i, 0)),
            ],
            out_specs=(
                pl.BlockSpec((soundings, blocks), lambda i, at: (0, 0)),
                pl.BlockSpec((hours, tiles, part), lambda i, at: (0, 0, 0)),
            ),
            scratch_shapes=[
                pltpu.VMEM((pages, LANES), jnp.float32),
                pltpu.VMEM((hours * tiles, chunk), jnp.bfloat16),
            ],
        ),
        out_shape=(
            jax.ShapeDtypeStruct((soundings, blocks), jnp.float32),
            jax.ShapeDtypeStruct((hours, tiles, part), jnp.float32),
        ),
        compiler_params=params,
        name="adjoint",
    )(at, sums, meta, feet)
    return modeled.T, gradient.transpose(1, 0, 2)


def solution(mesh):
    placed = (
        P(("flux", "obs"), None, None, None, None),
        P(("flux", "obs"), None),
        P(("flux", "obs"), None),
        P(),
        P("flux", None, None),
        P(("flux", "obs"), None),
        P(("flux", "obs"), None),
    )
    return jax.shard_map(
        shards,
        mesh=mesh,
        in_specs=placed,
        out_specs=(P(("flux", "obs"), None), P("flux", None, "obs")),
        check_vma=False,
    )
```

time: 360 us -> 147 us (0.41)
  waiting for transfers between devices: 252 us -> 93.9 us
  local copies, waits for them, and re-layouts: 38.9 us -> 2.8 us
  Pallas kernels: 0 us -> 19.7 us
  matrix products: 16.7 us -> 0 us
  other arithmetic: 14.7 us -> 0.08 us
  blocking collectives: 11.7 us -> 26.3 us
  between operations: 14.2 us -> 0.74 us
  starting transfers between devices: 10 us -> 3.58 us
    reduce_scatter x1 -> x0, waiting for transfers between devices: 81 us -> none  [shards(): lax.psum_scatter(local_sum, 'obs', scatter_dimension=2, tiled=True)]
    all_to_all x2 -> x1, waiting for transfers between devices: 171 us -> 93.9 us  [shards(): lax.all_to_all(send.reshape(devices, rows, part), both, split_axis=0, con...]
    gather x4 -> x0, local copies, waits for them, and re-layouts: 25.7 us -> none  [the longest x1 14.2 us: fetch_windows(): rows_taken = jnp.take(flux, jnp.maximum(wanted, 0), axis=0)]
    pallas_call x0 -> x3, Pallas kernels: none -> 19.7 us  [the longest x1 7.47 us: shards(): pl.pallas_call(functools.partial(adjoint_kernel, (rows, devices, states,...]
    dot_general x3 -> x0, matrix products: 16.7 us -> none  [the longest x1 9.34 us: accumulate(): jnp.dot(onehot, flattened, precision=lax.Precision.HIGHEST, preferred_ele...]
    all_to_all x1 -> x2, blocking collectives: 11.7 us -> 26.3 us  [the longest x1 14.5 us: shards(): lax.all_to_all(meta.reshape(devices, 4, rows), both, split_axis=0, concat...]
    mul x2 -> x0, other arithmetic: 12.6 us -> none  [the longest x1 9.07 us: shards(): jnp.take(gradients, source, axis=0)]
    all_to_all x3 -> x1, local copies, waits for them, and re-layouts: 11.5 us -> 0.01 us  [shards(): lax.all_to_all(meta.reshape(devices, 4, rows), both, split_axis=0, concat...]
  transfers between devices with their start and end apart: 3 -> 1, of which waited for: 3 -> 1; matrix products, arithmetic and copies ran while one was open for 0% -> 0% of each run, Pallas kernels for 0% -> 0%
where the time goes in v1:
time: 147 us
  waiting for transfers between devices  93.9 us (64%)
  blocking collectives  26.3 us (18%)
  Pallas kernels  19.7 us (13%)
  starting transfers between devices  3.58 us (2%)
  local copies, waits for them, and re-layouts  2.8 us (2%)
    all_to_all x1, waiting for transfers between devices, shards(): lax.all_to_all(send.reshape(devices, rows, part), both, split_axis=0, con...  93.9 us
    all_to_all x1, blocking collectives, shards(): lax.all_to_all(meta.reshape(devices, 4, rows), both, split_axis=0, concat...  14.5 us
    all_to_all x1, blocking collectives, shards(): sums = lax.all_to_all(sums, both, split_axis=0, concat_axis=0, tiled=True)  11.8 us
    pallas_call x1, Pallas kernels, shards(): pl.pallas_call(functools.partial(adjoint_kernel, (rows, devices, states,...  7.47 us
    pallas_call x1, Pallas kernels, shards(): pl.pallas_call(functools.partial(forward_kernel, (rows, copies, devices,...  6.25 us
    pallas_call x1, Pallas kernels, shards(): pl.pallas_call(functools.partial(pack_kernel, (owners, columns, capacity,...  5.94 us
    all_to_all x1, starting transfers between devices, shards(): lax.all_to_all(send.reshape(devices, rows, part), both, split_axis=0, con...  3.58 us
  transfers between devices with their start and end apart: 1, of which 1 were waited for; matrix products, arithmetic and copies ran while one was open for 0% of the time, Pallas kernels for 0%

profile of v1, /device:TPU:0, one launch (start us, length us, event | category | flops | bytes accessed | tf_op | source)
XLA Modules:
  0.0 147.1 jit_solution(5240998479245532577)
XLA Ops:
  0.6 0.0 copy-start.4
  0.6 0.0 copy-start.3
  0.7 0.0 copy-start.1
  0.7 0.0 copy-start
  0.7 0.0 copy-start.2
  0.7 2.8 %reshape.16.feet_ref = bf16[256,4096]{1,0:T(8,128)(2,1)S(1)} reshape(bf16[8,4,4,2,4096]{4,3,2,1,0:T(2,128)(2,1)} %param.7) | data formatting | bytes 4194304 | tf_op jit(solution)/shard_map/reshape | solution.py:215
  3.5 0.0 copy-done.4
  3.5 0.0 copy-done.3
  3.5 0.0 copy-done.1
  3.5 0.0 copy-done
  3.5 0.0 copy-done.2
  3.5 5.9 %pack.1 = (bf16[4,8,128,512]{3,2,1,0:T(8,128)(2,1)}, f32[4,8,4,128]{3,2,1,0:T(4,128)S(1)}) custom-call(s32[4,8]{1,0:T(4,128)S(1)} %bitcast.18, s32[512]{0:T(512)S(1)} %copy-done.1, s32[4,8]{1,0:T(4,128)S(1)} %bitcast.19, f32[4,8]{1,0:T(4,128)S(1)} %bitcast.20, f32[4,8]{1,0:T(4,128)S(1)} %bitcast.21, bf16[256,4096]{1,0:T(8,128)(2,1)S(1)} %reshape.16.feet_ref), custom_call_target="tpu_custom_call" | custom-call | tf_op jit(solution)/shard_map/pack/pallas_call | solution.py:188
  9.5 14.5 %all_to_all.15 = f32[32,4,128]{2,1,0:T(4,128)S(1)} all-to-all(f32[32,4,128]{2,1,0:T(4,128)S(1)} %bitcast.17), channel_id=1, replica_groups=mesh['flux'=4,'obs'=8] {'flux','obs'}, dimensions={0} | all-to-all | bytes 131072 | tf_op jit(solution)/shard_map/all_to_all | solution.py:220
  24.0 3.6 %all-to-all-start.1 = ((bf16[32,128,512]{2,1,0:T(8,128)(2,1)}), bf16[32,128,512]{2,1,0:T(8,128)(2,1)}, u32[]{:S(2)}, u32[]{:S(2)}) async-start(bf16[32,128,512]{2,1,0:T(8,128)(2,1)} %bitcast.23), calls=%async_computation.1 | async-start | bytes 8388608 | tf_op jit(solution)/shard_map/all_to_all | solution.py:217
  27.6 0.1 pad_add_fusion.at_ref
  27.6 93.9 %all-to-all-done.1 = bf16[32,128,512]{2,1,0:T(8,128)(2,1)} async-done(((bf16[32,128,512]{2,1,0:T(8,128)(2,1)}), bf16[32,128,512]{2,1,0:T(8,128)(2,1)}, u32[]{:S(2)}, u32[]{:S(2)}) %all-to-all-start.1) | async-done | bytes 4194336 | tf_op jit(solution)/shard_map/all_to_all | solution.py:217
  121.6 6.3 %forward.1 = f32[32,8,128]{2,1,0:T(8,128)S(1)} custom-call(s32[2]{0:T(128)S(1)} %pad_add_fusion.at_ref, f32[4,32,128]{2,1,0:T(8,128)S(1)} %bitcast.15, bf16[5,128,4096]{2,1,0:T(8,128)(2,1)} %bitcast.22, bf16[4096,512]{1,0:T(8,128)(2,1)} %bitcast.10.feet_ref), custom_call_target="tpu_custom_call" | custom-call | tf_op jit(solution)/shard_map/forward/pallas_call | solution.py:231
  127.8 11.8 %all_to_all.16.sums_ref = f32[32,8,128]{2,1,0:T(8,128)S(1)} all-to-all(f32[32,8,128]{2,1,0:T(8,128)S(1)} %forward.1), channel_id=1, replica_groups=mesh['flux'=4,'obs'=8] {'flux','obs'}, dimensions={0} | all-to-all | bytes 262144 | tf_op jit(solution)/shard_map/all_to_all | solution.py:249
  139.6 7.5 %adjoint.1 = (f32[4,8]{1,0:T(4,128)}, f32[5,128,512]{2,1,0:T(8,128)}) custom-call(s32[2]{0:T(128)S(1)} %pad_add_fusion.at_ref, f32[32,8,128]{2,1,0:T(8,128)S(1)} %all_to_all.16.sums_ref, f32[4,32,128]{2,1,0:T(8,128)S(1)} %bitcast.16, bf16[4096,512]{1,0:T(8,128)(2,1)} %bitcast.10.feet_ref), custom_call_target="tpu_custom_call" | custom-call | tf_op jit(solution)/shard_map/adjoint/pallas_call | solution.py:252
  (1 shorter events, 0.0 us)
Async XLA Ops:
  0.6 2.8 %copy-start.4 = (f32[8,4]{0,1:T(4,128)S(1)}, f32[8,4]{0,1:T(4,128)}, u32[]{:S(2)}) copy-start(f32[8,4]{0,1:T(4,128)} %param.13) | copy-start | bytes 388
  0.6 2.8 %copy-start.3 = (f32[8,4]{0,1:T(4,128)S(1)}, f32[8,4]{0,1:T(4,128)}, u32[]{:S(2)}) copy-start(f32[8,4]{0,1:T(4,128)} %param.12) | copy-start | bytes 388
  0.7 2.8 %copy-start.1 = (s32[512]{0:T(512)S(1)}, s32[512]{0:T(512)}, u32[]{:S(2)}) copy-start(s32[512]{0:T(512)} %row_ref.1) | copy-start | bytes 6148
  0.7 2.8 %copy-start = (s32[8,4]{0,1:T(4,128)S(1)}, s32[8,4]{0,1:T(4,128)}, u32[]{:S(2)}) copy-start(s32[8,4]{0,1:T(4,128)} %param.9) | copy-start | bytes 388
  0.7 2.8 %copy-start.2 = (s32[8,4]{0,1:T(4,128)S(1)}, s32[8,4]{0,1:T(4,128)}, u32[]{:S(2)}) copy-start(s32[8,4]{0,1:T(4,128)} %param.8) | copy-start | bytes 388
  24.0 97.6 %all-to-all-start.1 = ((bf16[32,128,512]{2,1,0:T(8,128)(2,1)}), bf16[32,128,512]{2,1,0:T(8,128)(2,1)}, u32[]{:S(2)}, u32[]{:S(2)}) async-start(bf16[32,128,512]{2,1,0:T(8,128)(2,1)} %bitcast.23), calls=%async_computation.1 | async-start | bytes 8388608 | tf_op jit(solution)/shard_map/all_to_all | solution.py:217

commit v2 on v0

v2 whole, which is shorter than its diff:
```python
import functools

import jax
import jax.numpy as jnp
from jax import lax
from jax.experimental import pallas as pl
from jax.experimental.pallas import tpu as pltpu
from jax.sharding import PartitionSpec as P

LANES = 128
VMEM_BYTES = 48 * 1024 * 1024
LEVELS = (5, 6, 7, 8, 9, 10, 12, 14, 16)


def iota(shape, dim):
    return lax.broadcasted_iota(jnp.int32, shape, dim)


def thirds(value):
    high = value.astype(jnp.bfloat16).astype(jnp.float32)
    rest = value - high
    middle = rest.astype(jnp.bfloat16).astype(jnp.float32)
    return high, middle, (rest - middle).astype(jnp.bfloat16).astype(jnp.float32)


class Sizes:
    def __init__(self, owners, columns, footprint, flux):
        self.owners, self.columns = owners, columns
        self.devices = owners * columns
        self.blocks, self.width, self.soundings, self.lags, cells = footprint
        self.tiles, self.hours = flux[0], flux[1]
        self.span = self.hours - self.lags + 1
        self.half = self.span * self.tiles // 2
        self.slots = self.blocks * self.width
        self.per_slot = self.soundings * self.lags
        self.part = cells // columns
        self.lane_tiles = self.part // LANES
        self.first = self.slots // owners
        self.rows = self.first * self.per_slot
        self.spill = self.slots // 2 * self.per_slot
        self.second = columns * self.first * self.per_slot
        self.notes = 8 * (self.second // self.part)
        self.states = self.blocks * self.soundings
        self.per_page = 8 * LANES // self.states
        self.pages = self.devices // self.per_page


def read_notes(sizes, notes, plane):
    lane = iota((1, notes.shape[1]), 1)
    inner = lax.rem(lane, jnp.int32(sizes.per_slot))
    base = notes[0:1]
    target = (base + sizes.half).astype(jnp.int32) + lax.rem(inner, jnp.int32(sizes.lags)) * sizes.tiles
    target = jnp.where(base > sizes.half - 0.5, -1, target)
    place = notes[1:2].astype(jnp.int32)
    block = lax.rem(place, jnp.int32(sizes.blocks))
    device = plane * sizes.columns + lax.div(place, jnp.int32(sizes.blocks))
    state = block * sizes.soundings + lax.div(inner, jnp.int32(sizes.lags))
    row = lax.div(device, jnp.int32(sizes.per_page)) * 8 + lax.rem(state, jnp.int32(8))
    column = lax.div(state, jnp.int32(8)) * sizes.per_page + lax.rem(device, jnp.int32(sizes.per_page))
    return target, row, column


def first_round(sizes, ref, step):
    sources, count = ref.shape[0], sizes.rows
    feet = jnp.concatenate(
        [
            ref[:, n * count : (n + 1) * count, :].reshape(sources * count, LANES)
            for n in range(sizes.lane_tiles)
        ],
        axis=1,
    )
    end = sizes.lane_tiles * count
    notes = jnp.concatenate(
        [ref[s, end : end + 8, :].astype(jnp.float32)[:, :count] for s in range(sources)], axis=1
    )
    lane = iota((1, sources * count), 1)
    plane = lax.div(step * sources + lax.div(lane, jnp.int32(count)), jnp.int32(sizes.columns))
    return feet, notes, plane


def second_round(sizes, ref):
    count = ref.shape[1] - sizes.notes
    notes = jnp.concatenate(
        [ref[0, n * 8 : (n + 1) * 8, :].astype(jnp.float32) for n in range(sizes.notes // 8)], axis=1
    )
    return ref[0, sizes.notes :, :], notes[:, :count]


def partial_sums(sizes, flux_ref, feet, notes, plane):
    target, row, column = read_notes(sizes, notes, plane)
    count = feet.shape[0]
    levels = sizes.hours * sizes.tiles
    products = lax.dot_general(
        flux_ref[...].reshape(levels, sizes.part),
        feet,
        (((1,), (1,)), ((), ())),
        preferred_element_type=jnp.float32,
    )
    chosen = jnp.where(iota((levels, count), 0) == target, products, 0.0)
    partial = jnp.sum(chosen, axis=0, keepdims=True)
    height = 8 * sizes.pages
    spread = jnp.where(iota((height, count), 0) == row, partial, 0.0)
    terms = jnp.concatenate(thirds(spread), axis=0).astype(jnp.bfloat16)
    lanes = (iota((LANES, count), 0) == column).astype(jnp.bfloat16)
    sums = lax.dot_general(
        terms, lanes, (((1,), (1,)), ((), ())), preferred_element_type=jnp.float32
    )
    return sums[:height] + sums[height : 2 * height] + sums[2 * height :]


def gradient_terms(sizes, model, feet, notes, plane):
    target, row, column = read_notes(sizes, notes, plane)
    count = feet.shape[0]
    height = 8 * sizes.pages
    lanes = (iota((LANES, count), 0) == column).astype(jnp.bfloat16)
    taken = jnp.dot(model, lanes, preferred_element_type=jnp.float32)
    taken = taken[:height] + taken[height : 2 * height] + taken[2 * height :]
    value = jnp.sum(
        jnp.where(iota((height, count), 0) == row, taken, 0.0), axis=0, keepdims=True
    )
    seen = notes[2:3] + notes[3:4] + notes[4:5]
    spread = notes[5:6] + notes[6:7] + notes[7:8]
    scaled = ((value - seen) / spread).astype(jnp.bfloat16).astype(jnp.float32)
    levels = sizes.hours * sizes.tiles
    coefficient = jnp.where(iota((levels, count), 0) == target, scaled, 0.0).astype(jnp.bfloat16)
    return jnp.dot(coefficient, feet, preferred_element_type=jnp.float32)


def pack_kernel(
    sizes, at_ref, list_ref, row_ref, hour_ref, seen_ref, var_ref, feet_ref, send_ref, *rest
):
    spills = rest[: sizes.columns]
    place, first_notes, spill_notes, count = rest[sizes.columns :]
    owners, per_slot = sizes.owners, sizes.per_slot
    step = pl.program_id(0)

    @pl.when(step == 0)
    def _():
        field, lane = iota((16, LANES), 0), iota((16, LANES), 1)
        inner = lane % per_slot
        sounding = inner // sizes.lags
        slot_at = lane // per_slot
        key_at = iota((1, sizes.slots * per_slot), 1)
        key = jnp.zeros(key_at.shape, jnp.int32)
        empty = jnp.where(field == 0, jnp.float32(sizes.half), 0.0)
        empty = jnp.where(field == 5, 1.0, jnp.where(field == 8, -1.0, empty))
        for o in range(owners):
            count[o] = 0
            first_notes[o] = empty[:8]
        count[owners] = 0
        left = empty
        for b in range(sizes.blocks):
            base = jnp.zeros(field.shape, jnp.float32)
            seen = jnp.zeros(field.shape, jnp.float32)
            spread = jnp.ones(field.shape, jnp.float32)
            for o in range(sizes.soundings):
                here = sounding == o
                hour = hour_ref[o, b] * sizes.tiles - sizes.half
                base = jnp.where(here, hour.astype(jnp.float32), base)
                seen = jnp.where(here, seen_ref[o, b], seen)
                spread = jnp.where(here, var_ref[o, b], spread)
            column = (b + sizes.blocks * at_ref[1]).astype(jnp.float32)
            pattern = jnp.where(field == 0, base, jnp.where(field == 1, column, 0.0))
            for n, term in enumerate(thirds(seen) + thirds(spread)):
                pattern = jnp.where(field == 2 + n, term, pattern)
            for k in range(sizes.width):
                stored = row_ref[list_ref[k, b]]
                owner = lax.div(stored, jnp.int32(sizes.tiles))
                tile = (stored - owner * sizes.tiles).astype(jnp.float32)
                position = count[owner]
                count[owner] = position + 1
                keep = position < sizes.first
                over = count[owners]
                count[owners] = over + jnp.where(keep, 0, 1)
                goes = jnp.where(
                    keep, owner * sizes.first + position, owners * sizes.first + over
                )
                value = jnp.where(field == 0, pattern + tile, pattern)
                value = jnp.where(field == 8, owner.astype(jnp.float32), value)
                value = jnp.where(
                    field == 9, (position - sizes.first).astype(jnp.float32), value
                )
                first_notes[owner] = jnp.where(
                    slot_at[:8] == jnp.where(keep, position, -1), value[:8], first_notes[owner]
                )
                left = jnp.where(slot_at == jnp.where(keep, -1, over), value, left)
                key = jnp.where(
                    key_at // per_slot == b * sizes.width + k,
                    goes * per_slot + key_at % per_slot,
                    key,
                )
        spill_notes[...] = left
        place[...] = (iota(place.shape, 0) == key).astype(jnp.bfloat16)

    packed = jnp.dot(place[...], feet_ref[...], preferred_element_type=jnp.float32)
    packed = packed.astype(jnp.bfloat16)
    rows = sizes.rows
    end = sizes.lane_tiles * rows
    for o in range(owners):
        for n in range(sizes.lane_tiles):
            send_ref[o, 0, n * rows : (n + 1) * rows, :] = packed[
                o * rows : (o + 1) * rows, n * LANES : (n + 1) * LANES
            ]
        send_ref[o, 0, end : end + 8, :] = first_notes[o].astype(jnp.bfloat16)
    for d in range(sizes.columns):

        @pl.when(step == d)
        def _():
            for n in range(sizes.lane_tiles):
                spills[d][n * sizes.spill : (n + 1) * sizes.spill, :] = packed[
                    owners * rows :, n * LANES : (n + 1) * LANES
                ]
            end = sizes.lane_tiles * sizes.spill
            spills[d][end : end + 16, :] = spill_notes[...].astype(jnp.bfloat16)


def regroup_kernel(sizes, *refs):
    spills = refs[: sizes.columns]
    send_ref, total_ref, feet, notes, place = refs[sizes.columns :]
    owner = pl.program_id(0)
    spill = sizes.spill
    end = sizes.lane_tiles * spill

    @pl.when(owner == 0)
    def _():
        for d, ref in enumerate(spills):
            for n in range(sizes.lane_tiles):
                feet[d * spill : (d + 1) * spill, n * LANES : (n + 1) * LANES] = ref[
                    n * spill : (n + 1) * spill, :
                ]
            notes[:, d * spill : (d + 1) * spill] = ref[end : end + 16, :].astype(jnp.float32)
        total_ref[...] = jnp.zeros_like(total_ref)

    mine = notes[8:9, :] == owner.astype(jnp.float32)
    total = jnp.zeros((1, 1), jnp.float32)
    keys = []
    for d in range(sizes.columns):
        here = mine[:, d * spill : (d + 1) * spill]
        position = total + notes[9:10, d * spill : (d + 1) * spill]
        inner = lax.rem(iota((1, spill), 1), jnp.int32(sizes.per_slot))
        keys.append(
            jnp.where(here, position.astype(jnp.int32) * sizes.per_slot + inner, -1)
        )
        total = total + jnp.sum(
            jnp.where(here, 1.0 / sizes.per_slot, 0.0), axis=1, keepdims=True
        )
    key = jnp.concatenate(keys, axis=1)
    place[...] = (iota(place.shape, 0) == key).astype(jnp.bfloat16)
    send_ref[0, sizes.notes :, :] = jnp.dot(
        place[...], feet[...], preferred_element_type=jnp.float32
    ).astype(jnp.bfloat16)
    moved = lax.dot_general(
        notes[0:8, :].astype(jnp.bfloat16),
        place[...],
        (((1,), (1,)), ((), ())),
        preferred_element_type=jnp.float32,
    )
    field, lane = iota(moved.shape, 0), iota(moved.shape, 1)
    empty = jnp.where(field == 0, jnp.float32(sizes.half), jnp.where(field == 5, 1.0, 0.0))
    moved = jnp.where(lane.astype(jnp.float32) < total * sizes.per_slot, moved, empty)
    moved = moved.astype(jnp.bfloat16)
    for n in range(sizes.notes // 8):
        send_ref[0, n * 8 : (n + 1) * 8, :] = moved[:, n * sizes.part : (n + 1) * sizes.part]
    total_ref[...] = jnp.maximum(total_ref[...], total)


def forward_first_kernel(sizes, at_ref, flux_ref, got_ref, out_ref):
    step = pl.program_id(0)
    feet, notes, plane = first_round(sizes, got_ref, step)
    sums = partial_sums(sizes, flux_ref, feet, notes, plane)

    @pl.when(step == 0)
    def _():
        out_ref[...] = sums

    @pl.when(step > 0)
    def _():
        out_ref[...] += sums


def forward_second_kernel(sizes, at_ref, flux_ref, got_ref, before_ref, out_ref, total):
    plane = pl.program_id(0)
    feet, notes = second_round(sizes, got_ref)
    sums = partial_sums(sizes, flux_ref, feet, notes, plane)

    @pl.when(plane == 0)
    def _():
        total[...] = before_ref[...] + sums

    @pl.when(plane > 0)
    def _():
        total[...] += sums

    @pl.when(plane == pl.num_programs(0) - 1)
    def _():
        out_ref[...] = jnp.broadcast_to(total[...][None], out_ref.shape)


def adjoint_kernel(
    sizes, chunks, at_ref, sums_ref, one_ref, two_ref, modeled_ref, grad_ref, model
):
    step = pl.program_id(0)

    @pl.when(step == 0)
    def _():
        sums = jnp.sum(sums_ref[...], axis=0)
        model[...] = jnp.concatenate(thirds(sums), axis=0).astype(jnp.bfloat16)
        me = at_ref[0]
        page, within = lax.div(me, sizes.per_page), lax.rem(me, sizes.per_page)
        lane = iota((8, LANES), 1)
        own = jnp.zeros((8, LANES), jnp.float32)
        for p in range(sizes.pages):
            own = jnp.where(page == p, sums[p * 8 : (p + 1) * 8], own)
        result = jnp.zeros(modeled_ref.shape, jnp.float32)
        at_block = iota(modeled_ref.shape, 1)
        each = 8 // sizes.soundings
        for q in range(sizes.states // 8):
            picked = jnp.where(lane == q * sizes.per_page + within, own, 0.0)
            column = jnp.sum(picked, axis=1, keepdims=True)
            for n in range(each):
                values = column[n * sizes.soundings : (n + 1) * sizes.soundings]
                result = jnp.where(at_block == q * each + n, values, result)
        modeled_ref[...] = result

    @pl.when(step < chunks)
    def _():
        feet, notes, plane = first_round(sizes, one_ref, step)
        terms = gradient_terms(sizes, model[...], feet, notes, plane).reshape(grad_ref.shape)

        @pl.when(step == 0)
        def _():
            grad_ref[...] = terms

        @pl.when(step > 0)
        def _():
            grad_ref[...] += terms

    @pl.when(step >= chunks)
    def _():
        feet, notes = second_round(sizes, two_ref)
        terms = gradient_terms(sizes, model[...], feet, notes, step - chunks)
        grad_ref[...] += terms.reshape(grad_ref.shape)


def shards(footprint, obs_hour, tile_list, tile_row, flux, observed, obs_var):
    sizes = Sizes(
        lax.axis_size("flux"), lax.axis_size("obs"), footprint.shape, flux.shape
    )
    owners, columns, devices, part = sizes.owners, sizes.columns, sizes.devices, sizes.part
    both = ("flux", "obs")
    params = pltpu.CompilerParams(vmem_limit_bytes=VMEM_BYTES)
    smem = pl.BlockSpec(memory_space=pltpu.SMEM)
    me = lax.axis_index("flux") * columns + lax.axis_index("obs")
    at = jnp.stack([me, lax.axis_index("obs")])
    flux = flux.transpose(1, 0, 2)

    first_height = sizes.lane_tiles * sizes.rows + 8
    spill_height = sizes.lane_tiles * sizes.spill + 16
    all_slots = sizes.slots * sizes.per_slot
    send, *spills = pl.pallas_call(
        functools.partial(pack_kernel, sizes),
        grid_spec=pltpu.PrefetchScalarGridSpec(
            num_scalar_prefetch=1,
            grid=(columns,),
            in_specs=[smem] * 5
            + [pl.BlockSpec((all_slots, part), lambda d, at: (0, d ^ at[1]))],
            out_specs=[
                pl.BlockSpec((owners, 1, first_height, LANES), lambda d, at: (0, d ^ at[1], 0, 0))
            ]
            + [pl.BlockSpec((spill_height, LANES), lambda d, at: (0, 0))] * columns,
            scratch_shapes=[
                pltpu.VMEM((owners * sizes.rows + sizes.spill, all_slots), jnp.bfloat16),
                pltpu.VMEM((owners, 8, LANES), jnp.float32),
                pltpu.VMEM((16, LANES), jnp.float32),
                pltpu.SMEM((owners + 1,), jnp.int32),
            ],
        ),
        out_shape=[jax.ShapeDtypeStruct((owners, columns, first_height, LANES), jnp.bfloat16)]
        + [jax.ShapeDtypeStruct((spill_height, LANES), jnp.bfloat16)] * columns,
        compiler_params=params,
        name="pack",
    )(
        at,
        tile_list.T,
        tile_row,
        obs_hour.T,
        observed.T,
        obs_var.T,
        footprint.reshape(all_slots, sizes.lane_tiles * columns * LANES),
    )
    got = lax.all_to_all(
        send.reshape(devices, first_height, LANES), both, split_axis=0, concat_axis=0, tiled=True
    )
    spills = spills[:1] + [
        lax.ppermute(spills[d], "obs", [(i, i ^ d) for i in range(columns)])
        for d in range(1, columns)
    ]
    second_height = sizes.notes + sizes.second
    send_second, total = pl.pallas_call(
        functools.partial(regroup_kernel, sizes),
        grid=(owners,),
        in_specs=[pl.BlockSpec((spill_height, LANES), lambda o: (0, 0))] * columns,
        out_specs=(
            pl.BlockSpec((1, second_height, part), lambda o: (o, 0, 0)),
            pl.BlockSpec((8, LANES), lambda o: (0, 0)),
        ),
        out_shape=(
            jax.ShapeDtypeStruct((owners, second_height, part), jnp.bfloat16),
            jax.ShapeDtypeStruct((8, LANES), jnp.float32),
        ),
        scratch_shapes=[
            pltpu.VMEM((columns * sizes.spill, part), jnp.bfloat16),
            pltpu.VMEM((16, columns * sizes.spill), jnp.float32),
            pltpu.VMEM((sizes.second, columns * sizes.spill), jnp.bfloat16),
        ],
        compiler_params=params,
        name="regroup",
    )(*spills)
    apart = 1
    while apart < owners:
        other = lax.ppermute(total, "flux", [(i, i ^ apart) for i in range(owners)])
        total = jnp.maximum(total, other)
        apart *= 2
    most = columns * sizes.first
    needed = total[0, 0]
    level = sum((needed > n * most // 16).astype(jnp.int32) for n in LEVELS[:-1])

    sources = min(devices, 1024 // sizes.rows)
    chunks = devices // sources
    copies = devices if devices <= 64 else 1
    height = 8 * sizes.pages
    flux_spec = pl.BlockSpec((sizes.hours, sizes.tiles, part), lambda i, at: (0, 0, at[1]))

    def finish(sixteenths):
        count = sizes.notes + sizes.second * sixteenths // 16

        def run(flux, got, send_second, at):
            got_second = lax.all_to_all(
                send_second[:, :count], "flux", split_axis=0, concat_axis=0, tiled=True
            )
            early = pl.pallas_call(
                functools.partial(forward_first_kernel, sizes),
                grid_spec=pltpu.PrefetchScalarGridSpec(
                    num_scalar_prefetch=1,
                    grid=(chunks,),
                    in_specs=[
                        flux_spec,
                        pl.BlockSpec((sources, first_height, LANES), lambda i, at: (i, 0, 0)),
                    ],
                    out_specs=pl.BlockSpec((height, LANES), lambda i, at: (0, 0)),
                ),
                out_shape=jax.ShapeDtypeStruct((height, LANES), jnp.float32),
                compiler_params=params,
                name="forward_first",
            )(at, flux, got)
            sums = pl.pallas_call(
                functools.partial(forward_second_kernel, sizes),
                grid_spec=pltpu.PrefetchScalarGridSpec(
                    num_scalar_prefetch=1,
                    grid=(owners,),
                    in_specs=[
                        flux_spec,
                        pl.BlockSpec((1, count, part), lambda i, at: (i, 0, 0)),
                        pl.BlockSpec((height, LANES), lambda i, at: (0, 0)),
                    ],
                    out_specs=pl.BlockSpec((copies, height, LANES), lambda i, at: (0, 0, 0)),
                    scratch_shapes=[pltpu.VMEM((height, LANES), jnp.float32)],
                ),
                out_shape=jax.ShapeDtypeStruct((copies, height, LANES), jnp.float32),
                compiler_params=params,
                name="forward_second",
            )(at, flux, got_second, early)
            if copies > 1:
                sums = lax.all_to_all(sums, both, split_axis=0, concat_axis=0, tiled=True)
            else:
                sums = lax.psum(sums, both)
            return pl.pallas_call(
                functools.partial(adjoint_kernel, sizes, chunks),
                grid_spec=pltpu.PrefetchScalarGridSpec(
                    num_scalar_prefetch=1,
                    grid=(chunks + owners,),
                    in_specs=[
                        pl.BlockSpec((copies, height, LANES), lambda i, at: (0, 0, 0)),
                        pl.BlockSpec(
                            (sources, first_height, LANES),
                            lambda i, at: (jnp.minimum(i, chunks - 1), 0, 0),
                        ),
                        pl.BlockSpec(
                            (1, count, part), lambda i, at: (jnp.maximum(i - chunks, 0), 0, 0)
                        ),
                    ],
                    out_specs=(
                        pl.BlockSpec((sizes.soundings, sizes.blocks), lambda i, at: (0, 0)),
                        pl.BlockSpec((sizes.hours, sizes.tiles, part), lambda i, at: (0, 0, 0)),
                    ),
                    scratch_shapes=[pltpu.VMEM((3 * height, LANES), jnp.bfloat16)],
                ),
                out_shape=(
                    jax.ShapeDtypeStruct((sizes.soundings, sizes.blocks), jnp.float32),
                    jax.ShapeDtypeStruct((sizes.hours, sizes.tiles, part), jnp.float32),
                ),
                compiler_params=params,
                name="adjoint",
            )(at, sums, got, got_second)

        return run

    modeled, gradient = lax.switch(
        level, [finish(n) for n in LEVELS], flux, got, send_second, at
    )
    return modeled.T, gradient.transpose(1, 0, 2)


def solution(mesh):
    placed = (
        P(("flux", "obs"), None, None, None, None),
        P(("flux", "obs"), None),
        P(("flux", "obs"), None),
        P(),
        P("flux", None, None),
        P(("flux", "obs"), None),
        P(("flux", "obs"), None),
    )
    return jax.shard_map(
        shards,
        mesh=mesh,
        in_specs=placed,
        out_specs=(P(("flux", "obs"), None), P("flux", None, "obs")),
        check_vma=False,
    )
```

time: 360 us -> 125 us (0.35)
  waiting for transfers between devices: 252 us -> 55.5 us
  local copies, waits for them, and re-layouts: 38.9 us -> 6.86 us
  Pallas kernels: 0 us -> 23.8 us
  matrix products: 16.7 us -> 0 us
  other arithmetic: 14.7 us -> 0.08 us
  starting transfers between devices: 10 us -> 20.9 us
  between operations: 14.2 us -> 5.94 us
    all_to_all x2, waiting for transfers between devices: 171 us -> 19.9 us  [the longest x1 19.9 us: run(): lax.all_to_all(send_second[:, :count], 'flux', split_axis=0, concat_axis=...]
    reduce_scatter x1 -> x0, waiting for transfers between devices: 81 us -> none  [shards(): lax.psum_scatter(local_sum, 'obs', scatter_dimension=2, tiled=True)]
    ppermute x0 -> x9, waiting for transfers between devices: none -> 35.6 us  [the longest x7 28.5 us: shards(): lax.ppermute(spills[d], 'obs', [(i, i ^ d) for i in range(columns)])]
    gather x4 -> x0, local copies, waits for them, and re-layouts: 25.7 us -> none  [the longest x1 14.2 us: fetch_windows(): rows_taken = jnp.take(flux, jnp.maximum(wanted, 0), axis=0)]
    pallas_call x0 -> x5, Pallas kernels: none -> 23.8 us  [the longest x1 6.17 us: run(): pl.pallas_call(functools.partial(adjoint_kernel, sizes, chunks), grid_spe...]
    dot_general x3 -> x0, matrix products: 16.7 us -> none  [the longest x1 9.34 us: accumulate(): jnp.dot(onehot, flattened, precision=lax.Precision.HIGHEST, preferred_ele...]
    mul x2 -> x0, other arithmetic: 12.6 us -> none  [the longest x1 9.07 us: shards(): jnp.take(gradients, source, axis=0)]
    all_to_all x3 -> x0, local copies, waits for them, and re-layouts: 11.5 us -> none  [the longest x1 5.72 us: shards(): lax.all_to_all(outgoing.reshape(owners, capacity, hour_count, cell_count)...]
  transfers between devices with their start and end apart: 3 -> 11, of which waited for: 3 -> 7; matrix products, arithmetic and copies ran while one was open for 0% -> 0% of each run, Pallas kernels for 0% -> 7%
where the time goes in v2:
time: 125 us
  waiting for transfers between devices  55.5 us (44%)
  Pallas kernels  23.8 us (19%)
  starting transfers between devices  20.9 us (17%)
  blocking collectives  11.4 us (9%)
  local copies, waits for them, and re-layouts  6.86 us (5%)
  between operations  5.94 us (5%)
    ppermute x7, waiting for transfers between devices, shards(): lax.ppermute(spills[d], 'obs', [(i, i ^ d) for i in range(columns)])  28.5 us
    all_to_all x1, waiting for transfers between devices, run(): lax.all_to_all(send_second[:, :count], 'flux', split_axis=0, concat_axis=...  19.9 us
    all_to_all x1, blocking collectives, run(): sums = lax.all_to_all(sums, both, split_axis=0, concat_axis=0, tiled=True)  11.4 us
    all_to_all x1, starting transfers between devices, shards(): lax.all_to_all(send.reshape(devices, first_height, LANES), both, split_ax...  7.3 us
    ppermute x2, waiting for transfers between devices, shards(): other = lax.ppermute(total, 'flux', [(i, i ^ apart) for i in range(owners)])  7.05 us
    ppermute x7, starting transfers between devices, shards(): lax.ppermute(spills[d], 'obs', [(i, i ^ d) for i in range(columns)])  6.71 us
    pallas_call x1, Pallas kernels, run(): pl.pallas_call(functools.partial(adjoint_kernel, sizes, chunks), grid_spe...  6.17 us
    pallas_call x1, Pallas kernels, shards(): pl.pallas_call(functools.partial(pack_kernel, sizes), grid_spec=pltpu.Pre...  4.97 us
  transfers between devices with their start and end apart: 11, of which 7 were waited for; matrix products, arithmetic and copies ran while one was open for 0% of the time, Pallas kernels for 7%

profile of v2, /device:TPU:0, one launch (start us, length us, event | category | flops | bytes accessed | tf_op | source)
XLA Modules:
  0.0 124.5 jit_solution(2728557819976609385)
XLA Ops:
  0.6 0.0 copy-start.1
  0.6 0.0 copy-start.2
  0.7 0.0 copy-start.3
  0.7 0.0 copy-start.4
  0.7 0.0 copy-start.5
  0.7 2.8 %reshape.41.feet_ref = bf16[256,4096]{1,0:T(8,128)(2,1)S(1)} reshape(bf16[8,4,4,2,4096]{4,3,2,1,0:T(2,128)(2,1)} %param.16) | data formatting | bytes 4194304 | tf_op jit(solution)/shard_map/reshape | solution.py:389
  3.5 0.1 pad_add_fusion.at_ref
  3.6 0.0 copy-done.1
  3.6 0.0 copy-done.2
  3.6 0.0 copy-done.3
  3.6 0.0 copy-done.4
  3.6 0.0 copy-done.5
  3.6 5.0 %pack.1 = (bf16[4,8,264,128]{3,2,1,0:T(8,128)(2,1)S(1)}, bf16[528,128]{1,0:T(8,128)(2,1)S(1)}, bf16[528,128]{1,0:T(8,128)(2,1)S(1)}, bf16[528,128]{1,0:T(8,128)(...) custom-call(s32[2]{0:T(128)S(1)} %pad_add_fusion.at_ref, ...), custom_call_target="tpu_custom_call" | custom-call | tf_op jit(solution)/shard_map/pack/pallas_call | solution.py:360
  8.5 0.0 copy-start
  8.6 1.4 %copy-done = bf16[4,8,264,128]{3,2,1,0:T(8,128)(2,1)} copy-done((bf16[4,8,264,128]{3,2,1,0:T(8,128)(2,1)}, bf16[4,8,264,128]{3,2,1,0:T(8,128)(2,1)S(1)}, u32[]{:S(2)}) %copy-start) | copy-done | bytes 2162712
  9.9 7.3 %all-to-all-start.18 = ((bf16[32,264,128]{2,1,0:T(8,128)(2,1)}), bf16[32,264,128]{2,1,0:T(8,128)(2,1)S(1)}, u32[]{:S(2)}, u32[]{:S(2)}) async-start(bf16[32,264,128]{2,1,0:T(8,128)(2,1)} %bitcast.11), calls=%async_computation.18 | async-start | bytes 4325376 | tf_op jit(solution)/shard_map/all_to_all | solution.py:391
  17.2 0.3 collective-permute-start
  17.5 1.7 %collective-permute-start.1 = (bf16[528,128]{1,0:T(8,128)(2,1)S(1)}, bf16[528,128]{1,0:T(8,128)(2,1)S(1)}, u32[]{:S(2)}, u32[]{:S(2)}) collective-permute-start(bf16[528,128]{1,0:T(8,128)(2,1)S(1)} %get-tuple-element.125), channel_id=1, source_target_pairs={{0,2},{1,3},{2,0},{3,1},{4,6},{5,7},{6,4},{7,5},{8,10},{9,11},{10,... | collective-permute-start | bytes 405512 | tf_op jit(solution)/shard_map/ppermute | solution.py:395
  19.2 0.0 collective-permute-start.2
  19.2 1.7 %collective-permute-start.3 = (bf16[528,128]{1,0:T(8,128)(2,1)S(1)}, bf16[528,128]{1,0:T(8,128)(2,1)S(1)}, u32[]{:S(2)}, u32[]{:S(2)}) collective-permute-start(bf16[528,128]{1,0:T(8,128)(2,1)S(1)} %get-tuple-element.127), channel_id=1, source_target_pairs={{0,4},{1,5},{2,6},{3,7},{4,0},{5,1},{6,2},{7,3},{8,12},{9,13},{10,... | collective-permute-start | bytes 405512 | tf_op jit(solution)/shard_map/ppermute | solution.py:395
  20.9 0.1 collective-permute-start.4
  21.0 0.0 collective-permute-done.refs_1_
  21.0 2.6 %collective-permute-start.5 = (bf16[528,128]{1,0:T(8,128)(2,1)S(1)}, bf16[528,128]{1,0:T(8,128)(2,1)S(1)}, u32[]{:S(2)}, u32[]{:S(2)}) collective-permute-start(bf16[528,128]{1,0:T(8,128)(2,1)S(1)} %get-tuple-element.129), channel_id=1, source_target_pairs={{0,6},{1,7},{2,4},{3,5},{4,2},{5,3},{6,0},{7,1},{8,14},{9,15},{10,... | collective-permute-start | bytes 405512 | tf_op jit(solution)/shard_map/ppermute | solution.py:395
  23.6 13.5 %collective-permute-done.1.refs_2_ = bf16[528,128]{1,0:T(8,128)(2,1)S(1)} collective-permute-done((bf16[528,128]{1,0:T(8,128)(2,1)S(1)}, bf16[528,128]{1,0:T(8,128)(2,1)S(1)}, u32[]{:S(2)}, u32[]{:S(2)}) %collective-permute-start.1) | collective-permute-done | bytes 135200 | tf_op jit(solution)/shard_map/ppermute | solution.py:395
  37.1 0.3 collective-permute-start.6
  37.4 4.5 %collective-permute-done.2.refs_3_ = bf16[528,128]{1,0:T(8,128)(2,1)S(1)} collective-permute-done((bf16[528,128]{1,0:T(8,128)(2,1)S(1)}, bf16[528,128]{1,0:T(8,128)(2,1)S(1)}, u32[]{:S(2)}, u32[]{:S(2)}) %collective-permute-start.2) | collective-permute-done | bytes 135200 | tf_op jit(solution)/shard_map/ppermute | solution.py:395
  42.0 0.0 collective-permute-done.3.refs_4_
  42.0 0.0 collective-permute-done.4.refs_5_
  42.0 8.3 %collective-permute-done.5.refs_6_ = bf16[528,128]{1,0:T(8,128)(2,1)S(1)} collective-permute-done((bf16[528,128]{1,0:T(8,128)(2,1)S(1)}, bf16[528,128]{1,0:T(8,128)(2,1)S(1)}, u32[]{:S(2)}, u32[]{:S(2)}) %collective-permute-start.5) | collective-permute-done | bytes 135200 | tf_op jit(solution)/shard_map/ppermute | solution.py:395
  50.2 2.2 %collective-permute-done.6.refs_7_ = bf16[528,128]{1,0:T(8,128)(2,1)S(1)} collective-permute-done((bf16[528,128]{1,0:T(8,128)(2,1)S(1)}, bf16[528,128]{1,0:T(8,128)(2,1)S(1)}, u32[]{:S(2)}, u32[]{:S(2)}) %collective-permute-start.6) | collective-permute-done | bytes 135200 | tf_op jit(solution)/shard_map/ppermute | solution.py:395
  52.5 4.9 %regroup.1 = (bf16[4,520,512]{2,1,0:T(8,128)(2,1)}, f32[8,128]{1,0:T(8,128)S(1)}) custom-call(bf16[528,128]{1,0:T(8,128)(2,1)S(1)} %get-tuple-element.123.refs_0_, bf16[528,128]{1,0:T(8,128)(2,1)S(1)} %collective-permute-done.refs_1_, bf16[528,128]{1,0:T(8,128)(2,1)S(1)} %collective-permute-done.1.refs_2_, ...), custom_call_target="tpu_custom_call" | custom-call | tf_op jit(solution)/shard_map/regroup/pallas_call | solution.py:399
  57.4 0.6 collective-permute-start.7
  58.0 3.0 %collective-permute-done.7 = f32[8,128]{1,0:T(8,128)S(1)} collective-permute-done((f32[8,128]{1,0:T(8,128)S(1)}, f32[8,128]{1,0:T(8,128)S(1)}, u32[]{:S(2)}, u32[]{:S(2)}) %collective-permute-start.7) | collective-permute-done | bytes 4128 | tf_op jit(solution)/shard_map/ppermute | solution.py:421
  61.0 2.8 %collective-permute-start.8 = (f32[8,128]{1,0:T(8,128)S(1)}, f32[8,128]{1,0:T(8,128)S(1)}, u32[]{:S(2)}, u32[]{:S(2)}) collective-permute-start(f32[8,128]{1,0:T(8,128)S(1)} %max.6), channel_id=1, source_target_pairs={{0,16},{8,24},{16,0},{24,8},{1,17},{9,25},{17,1},{25,9},{2,18},{10... | collective-permute-start | bytes 12296 | tf_op jit(solution)/shard_map/ppermute | solution.py:421
  63.8 4.0 %collective-permute-done.8 = f32[8,128]{1,0:T(8,128)S(1)} collective-permute-done((f32[8,128]{1,0:T(8,128)S(1)}, f32[8,128]{1,0:T(8,128)S(1)}, u32[]{:S(2)}, u32[]{:S(2)}) %collective-permute-start.8) | collective-permute-done | bytes 4128 | tf_op jit(solution)/shard_map/ppermute | solution.py:421
  67.9 0.5 slice.27
  73.6 0.0 all-to-all-done.18
  73.6 51.0 %conditional.1 = ((f32[4,8]{1,0:T(4,128)}, f32[5,128,512]{2,1,0:T(8,128)})) conditional(s32[]{:T(128)} %bitcast.6, (bf16[4,520,512]{2,1,0:T(8,128)(2,1)}, s32[2]{0:T(128)S(1)}, bf16[5,128,4096]{2,1,0:T(8,128)(2,1)}, bf16[32,264,128]{2,1,0:T(8,128)(2,1)S(1)}) %tuple.55, (bf16[4,520,512]{2,1,0:T(8,128)(2,1)}, ...), branch_computations={%region_0.0_spmd, %region_1.0_spmd, %region_2.0_spmd, %region_3.0_... | conditional | bytes 26902624 | solution.py:508
  73.6 2.2 %slice.20 = bf16[4,232,512]{2,1,0:T(8,128)(2,1)} slice(bf16[4,520,512]{2,1,0:T(8,128)(2,1)} %get-tuple-element.82), slice={[0:4], [0:232], [0:512]} | slice | bytes 1900544 | tf_op jit(solution)/shard_map/cond/branch_2_fun/slice | solution.py:439
  75.8 3.5 %all-to-all-start.4 = ((bf16[4,232,512]{2,1,0:T(8,128)(2,1)}), bf16[4,232,512]{2,1,0:T(8,128)(2,1)S(1)}, u32[]{:S(2)}, u32[]{:S(2)}) async-start(bf16[4,232,512]{2,1,0:T(8,128)(2,1)} %slice.20), calls=%async_computation.4 | async-start | bytes 1900544 | tf_op jit(solution)/shard_map/cond/branch_2_fun/all_to_all | solution.py:438
  79.3 3.8 %forward_first.11.before_ref = f32[8,128]{1,0:T(8,128)S(1)} custom-call(s32[2]{0:T(128)S(1)} %get-tuple-element.80.at_ref, bf16[5,128,4096]{2,1,0:T(8,128)(2,1)} %get-tuple-element.81.flux_ref, bf16[32,264,128]{2,1,0:T(8,128)(2,1)S(1)} %get-tuple-element.83.got_ref.one_ref), custom_call_target="tpu_custom_call" | custom-call | tf_op jit(solution)/shard_map/cond/branch_2_fun/forward_first/pallas_call | solution.py:441
  83.1 19.9 %all-to-all-done.4.got_ref.two_ref = bf16[4,232,512]{2,1,0:T(8,128)(2,1)S(1)} async-done(((bf16[4,232,512]{2,1,0:T(8,128)(2,1)}), bf16[4,232,512]{2,1,0:T(8,128)(2,1)S(1)}, u32[]{:S(2)}, u32[]{:S(2)}) %all-to-all-start.4) | async-done | bytes 950304 | tf_op jit(solution)/shard_map/cond/branch_2_fun/all_to_all | solution.py:438
  103.0 4.0 %forward_second.11 = f32[32,8,128]{2,1,0:T(8,128)S(1)} custom-call(s32[2]{0:T(128)S(1)} %get-tuple-element.80.at_ref, bf16[5,128,4096]{2,1,0:T(8,128)(2,1)} %get-tuple-element.81.flux_ref, bf16[4,232,512]{2,1,0:T(8,128)(2,1)S(1)} %all-to-all-done.4.got_ref.two_ref, f32[8,128]{1,0:T(8,128)S(1)} %forward_first.11.before_ref), custom_call_target="tpu_custom_call" | custom-call | tf_op jit(solution)/shard_map/cond/branch_2_fun/forward_second/pallas_call | solution.py:456
  107.0 11.4 %all_to_all.79.sums_ref = f32[32,8,128]{2,1,0:T(8,128)S(1)} all-to-all(f32[32,8,128]{2,1,0:T(8,128)S(1)} %forward_second.11), channel_id=1, replica_groups=mesh['flux'=4,'obs'=8] {'flux','obs'}, dimensions={0} | all-to-all | bytes 262144 | tf_op jit(solution)/shard_map/cond/branch_2_fun/all_to_all | solution.py:474
  118.4 6.2 %adjoint.11 = (f32[4,8]{1,0:T(4,128)}, f32[5,128,512]{2,1,0:T(8,128)}) custom-call(s32[2]{0:T(128)S(1)} %get-tuple-element.80.at_ref, f32[32,8,128]{2,1,0:T(8,128)S(1)} %all_to_all.79.sums_ref, bf16[32,264,128]{2,1,0:T(8,128)(2,1)S(1)} %get-tuple-element.83.got_ref.one_ref, bf16[4,232,512]{2,1,0:T(8,128)(2,1)S(1)} %all-to-all-done.4.got_ref.two_ref), custom_call_target="tpu_custom_call" | custom-call | tf_op jit(solution)/shard_map/cond/branch_2_fun/adjoint/pallas_call | solution.py:477
  (2 shorter events, 0.0 us)
Async XLA Ops:
  0.6 2.9 %copy-start.1 = (s32[8,4]{0,1:T(4,128)S(1)}, s32[8,4]{0,1:T(4,128)}, u32[]{:S(2)}) copy-start(s32[8,4]{0,1:T(4,128)} %param.18) | copy-start | bytes 388
  0.6 2.9 %copy-start.2 = (s32[512]{0:T(512)S(1)}, s32[512]{0:T(512)}, u32[]{:S(2)}) copy-start(s32[512]{0:T(512)} %row_ref.1) | copy-start | bytes 6148
  0.7 2.9 %copy-start.3 = (s32[8,4]{0,1:T(4,128)S(1)}, s32[8,4]{0,1:T(4,128)}, u32[]{:S(2)}) copy-start(s32[8,4]{0,1:T(4,128)} %param.17) | copy-start | bytes 388
  0.7 2.9 %copy-start.4 = (f32[8,4]{0,1:T(4,128)S(1)}, f32[8,4]{0,1:T(4,128)}, u32[]{:S(2)}) copy-start(f32[8,4]{0,1:T(4,128)} %param.21) | copy-start | bytes 388
  0.7 2.9 %copy-start.5 = (f32[8,4]{0,1:T(4,128)S(1)}, f32[8,4]{0,1:T(4,128)}, u32[]{:S(2)}) copy-start(f32[8,4]{0,1:T(4,128)} %param.22) | copy-start | bytes 388
  8.5 1.4 %copy-start = (bf16[4,8,264,128]{3,2,1,0:T(8,128)(2,1)}, bf16[4,8,264,128]{3,2,1,0:T(8,128)(2,1)S(1)}, u32[]{:S(2)}) copy-start(bf16[4,8,264,128]{3,2,1,0:T(8,128)(2,1)S(1)} %get-tuple-element.133) | copy-start | bytes 6488068
  9.9 63.6 %all-to-all-start.18 = ((bf16[32,264,128]{2,1,0:T(8,128)(2,1)}), bf16[32,264,128]{2,1,0:T(8,128)(2,1)S(1)}, u32[]{:S(2)}, u32[]{:S(2)}) async-start(bf16[32,264,128]{2,1,0:T(8,128)(2,1)} %bitcast.11), calls=%async_computation.18 | async-start | bytes 4325376 | tf_op jit(solution)/shard_map/all_to_all | solution.py:391
  17.2 3.8 %collective-permute-start = (bf16[528,128]{1,0:T(8,128)(2,1)S(1)}, bf16[528,128]{1,0:T(8,128)(2,1)S(1)}, u32[]{:S(2)}, u32[]{:S(2)}) collective-permute-start(bf16[528,128]{1,0:T(8,128)(2,1)S(1)} %get-tuple-element.124), channel_id=1, source_target_pairs={{0,1},{1,0},{2,3},{3,2},{4,5},{5,4},{6,7},{7,6},{8,9},{9,8},{10,11... | collective-permute-start | bytes 405512 | tf_op jit(solution)/shard_map/ppermute | solution.py:395
  17.5 19.6 %collective-permute-start.1 = (bf16[528,128]{1,0:T(8,128)(2,1)S(1)}, bf16[528,128]{1,0:T(8,128)(2,1)S(1)}, u32[]{:S(2)}, u32[]{:S(2)}) collective-permute-start(bf16[528,128]{1,0:T(8,128)(2,1)S(1)} %get-tuple-element.125), channel_id=1, source_target_pairs={{0,2},{1,3},{2,0},{3,1},{4,6},{5,7},{6,4},{7,5},{8,10},{9,11},{10,... | collective-permute-start | bytes 405512 | tf_op jit(solution)/shard_map/ppermute | solution.py:395
  19.2 22.8 %collective-permute-start.2 = (bf16[528,128]{1,0:T(8,128)(2,1)S(1)}, bf16[528,128]{1,0:T(8,128)(2,1)S(1)}, u32[]{:S(2)}, u32[]{:S(2)}) collective-permute-start(bf16[528,128]{1,0:T(8,128)(2,1)S(1)} %get-tuple-element.126), channel_id=1, source_target_pairs={{0,3},{1,2},{2,1},{3,0},{4,7},{5,6},{6,5},{7,4},{8,11},{9,10},{10,... | collective-permute-start | bytes 405512 | tf_op jit(solution)/shard_map/ppermute | solution.py:395
  19.2 22.8 %collective-permute-start.3 = (bf16[528,128]{1,0:T(8,128)(2,1)S(1)}, bf16[528,128]{1,0:T(8,128)(2,1)S(1)}, u32[]{:S(2)}, u32[]{:S(2)}) collective-permute-start(bf16[528,128]{1,0:T(8,128)(2,1)S(1)} %get-tuple-element.127), channel_id=1, source_target_pairs={{0,4},{1,5},{2,6},{3,7},{4,0},{5,1},{6,2},{7,3},{8,12},{9,13},{10,... | collective-permute-start | bytes 405512 | tf_op jit(solution)/shard_map/ppermute | solution.py:395
  20.9 21.1 %collective-permute-start.4 = (bf16[528,128]{1,0:T(8,128)(2,1)S(1)}, bf16[528,128]{1,0:T(8,128)(2,1)S(1)}, u32[]{:S(2)}, u32[]{:S(2)}) collective-permute-start(bf16[528,128]{1,0:T(8,128)(2,1)S(1)} %get-tuple-element.128), channel_id=1, source_target_pairs={{0,5},{1,4},{2,7},{3,6},{4,1},{5,0},{6,3},{7,2},{8,13},{9,12},{10,... | collective-permute-start | bytes 405512 | tf_op jit(solution)/shard_map/ppermute | solution.py:395
  21.0 29.2 %collective-permute-start.5 = (bf16[528,128]{1,0:T(8,128)(2,1)S(1)}, bf16[528,128]{1,0:T(8,128)(2,1)S(1)}, u32[]{:S(2)}, u32[]{:S(2)}) collective-permute-start(bf16[528,128]{1,0:T(8,128)(2,1)S(1)} %get-tuple-element.129), channel_id=1, source_target_pairs={{0,6},{1,7},{2,4},{3,5},{4,2},{5,3},{6,0},{7,1},{8,14},{9,15},{10,... | collective-permute-start | bytes 405512 | tf_op jit(solution)/shard_map/ppermute | solution.py:395
  37.1 15.4 %collective-permute-start.6 = (bf16[528,128]{1,0:T(8,128)(2,1)S(1)}, bf16[528,128]{1,0:T(8,128)(2,1)S(1)}, u32[]{:S(2)}, u32[]{:S(2)}) collective-permute-start(bf16[528,128]{1,0:T(8,128)(2,1)S(1)} %get-tuple-element.130), channel_id=1, source_target_pairs={{0,7},{1,6},{2,5},{3,4},{4,3},{5,2},{6,1},{7,0},{8,15},{9,14},{10,... | collective-permute-start | bytes 405512 | tf_op jit(solution)/shard_map/ppermute | solution.py:395
  57.4 3.7 %collective-permute-start.7 = (f32[8,128]{1,0:T(8,128)S(1)}, f32[8,128]{1,0:T(8,128)S(1)}, u32[]{:S(2)}, u32[]{:S(2)}) collective-permute-start(f32[8,128]{1,0:T(8,128)S(1)} %get-tuple-element.131), channel_id=1, source_target_pairs={{0,8},{8,0},{16,24},{24,16},{1,9},{9,1},{17,25},{25,17},{2,10},{10... | collective-permute-start | bytes 12296 | tf_op jit(solution)/shard_map/ppermute | solution.py:421
  61.0 6.8 %collective-permute-start.8 = (f32[8,128]{1,0:T(8,128)S(1)}, f32[8,128]{1,0:T(8,128)S(1)}, u32[]{:S(2)}, u32[]{:S(2)}) collective-permute-start(f32[8,128]{1,0:T(8,128)S(1)} %max.6), channel_id=1, source_target_pairs={{0,16},{8,24},{16,0},{24,8},{1,17},{9,25},{17,1},{25,9},{2,18},{10... | collective-permute-start | bytes 12296 | tf_op jit(solution)/shard_map/ppermute | solution.py:421
  75.8 27.2 %all-to-all-start.4 = ((bf16[4,232,512]{2,1,0:T(8,128)(2,1)}), bf16[4,232,512]{2,1,0:T(8,128)(2,1)S(1)}, u32[]{:S(2)}, u32[]{:S(2)}) async-start(bf16[4,232,512]{2,1,0:T(8,128)(2,1)} %slice.20), calls=%async_computation.4 | async-start | bytes 1900544 | tf_op jit(solution)/shard_map/cond/branch_2_fun/all_to_all | solution.py:438
